TPU v7x, 512 devices: a whole 4x4x16 slice. The times are simulated.
512 devices in a mesh: seq: 64 (over z, x), head: 8 (over y, core).
Axes of the slice: x: 4, y: 4, z: 16, core: 2. Of those that a mesh axis runs over, the one named last changes fastest.
Arguments:
- queries: bfloat16 [32768, 2048], P(('seq', 'head')), may hold values from -6 to 6
- keys: bfloat16 [32768, 2048], P(('seq', 'head')), may hold values from -6 to 6
- values: bfloat16 [32768, 4096], P(('seq', 'head')), may hold values from -6 to 6
- in_gate: float32 [8, 32768], P('head', 'seq'), may hold values from -8 to 130
- forget_gate: float32 [8, 32768], P('head', 'seq'), may hold values from -0.1 to 14
- out_gate: bfloat16 [32768, 4096], P(('seq', 'head')), may hold values from -6 to 6
Outputs:
- layer_output: bfloat16 [32768, 4096], P(('seq', 'head'))
All inputs are finite; a program needn't handle non-finite values.
Results may differ from a plain program's by a relative error of at most 0.0065.
Values may be sent and summed in bfloat16 or wider, within the bound.
A program may use at most 128 MiB of HBM per device.

v0:
```python
import jax
import jax.numpy as jnp
from jax import lax
from jax.sharding import PartitionSpec as P

NEG_FILL = -1e30


def prefix(part, axis, combine, identity):
    place = lax.axis_index(axis)
    gathered = jax.tree.map(lambda a: lax.all_gather(a, axis), part)
    state = jax.tree.map(lambda a, e: jnp.zeros_like(a) + jnp.asarray(e, a.dtype), part, identity)

    def one(lap, state):
        return combine(
            state, jax.tree.map(lambda a: lax.dynamic_index_in_dim(a, lap, 0, False), gathered)
        )

    return lax.fori_loop(0, place, one, state)


def merge_states(earlier, later):
    decay_one, memory_one, normal_one, peak_one = earlier
    decay_two, memory_two, normal_two, peak_two = later
    peak_new = jnp.maximum(decay_two + peak_one, peak_two)
    scale_one = jnp.exp(decay_two + peak_one - peak_new)
    scale_two = jnp.exp(peak_two - peak_new)
    memory_new = scale_one[:, None, None] * memory_one + scale_two[:, None, None] * memory_two
    normal_new = scale_one[:, None] * normal_one + scale_two[:, None] * normal_two
    return (decay_one + decay_two, memory_new, normal_new, peak_new)


def per_device(queries, keys, values, in_gate, forget_gate, out_gate):
    groups = lax.axis_size("head")
    heads_dev = in_gate.shape[0]
    tok_rows = queries.shape[0]
    key_dim = queries.shape[1] // (groups * heads_dev)
    value_dim = values.shape[1] // (groups * heads_dev)
    block_rows = tok_rows * groups
    query_tok = queries.reshape(tok_rows, groups, heads_dev * key_dim)
    key_tok = keys.reshape(tok_rows, groups, heads_dev * key_dim)
    value_tok = values.reshape(tok_rows, groups, heads_dev * value_dim)
    query_all, key_all, value_everything = (
        lax.all_to_all(query_tok, "head", split_axis=1, concat_axis=0, tiled=True),
        lax.all_to_all(key_tok, "head", split_axis=1, concat_axis=0, tiled=True),
        lax.all_to_all(value_tok, "head", split_axis=1, concat_axis=0, tiled=True),
    )
    log_keep = jax.nn.log_sigmoid(forget_gate)
    within = jnp.cumsum(log_keep, axis=1)
    decay_total = within[:, -1]
    since_end = decay_total[:, None] - within + in_gate
    peak_own = jnp.max(since_end, axis=1)
    weight = jnp.exp(since_end - peak_own[:, None])
    weighted_product = weight.T[:, :, None] * key_all
    memory_own = jnp.einsum(
        "mlj,mln->ljn",
        weighted_product.astype(jnp.bfloat16),
        value_everything,
        preferred_element_type=jnp.float32,
    )
    normal_own = jnp.sum(weighted_product, axis=0)
    own_summary = (decay_total, memory_own, normal_own, peak_own)
    identity_state = (
        jnp.zeros_like(decay_total),
        jnp.zeros_like(memory_own),
        jnp.zeros_like(normal_own),
        jnp.full_like(peak_own, NEG_FILL),
    )
    incoming = prefix(own_summary, "seq", merge_states, identity_state)
    decay_in, memory_incoming, normal_in, peak_in = incoming
    scale = key_dim ** (-0.5)
    positions = jnp.arange(block_rows)
    entry_log = within + peak_in[:, None]
    local_log = within[:, :, None] - within[:, None, :] + in_gate[:, None, :]
    causal = positions[None, :] <= positions[:, None]
    local_log = jnp.where(causal[None], local_log, -jnp.inf)
    scores = (
        jnp.einsum("rhk,shk->hrs", query_all, key_all, preferred_element_type=jnp.float32) * scale
    )
    query_expanded = query_all.astype(jnp.float32) * scale
    from_memory = jnp.einsum(
        "xcs,cse->xce", query_expanded, memory_incoming, precision=lax.Precision.HIGHEST
    )
    from_normal = jnp.einsum(
        "rhk,hk->hr", query_expanded, normal_in, precision=lax.Precision.HIGHEST
    )
    peak_row = jnp.maximum(entry_log, jnp.max(local_log, axis=2))
    mixing = jnp.exp(local_log - peak_row[:, :, None]) * scores
    entry_scale = jnp.exp(entry_log - peak_row)
    numerator = jnp.einsum(
        "hrs,shv->rhv",
        mixing.astype(jnp.bfloat16),
        value_everything,
        preferred_element_type=jnp.float32,
    )
    numerator = numerator + entry_scale.T[:, :, None] * from_memory
    denominator = jnp.sum(mixing, axis=2) + entry_scale * from_normal
    floor_row = jnp.maximum(jnp.abs(denominator), 1.0)
    pieces = (numerator / floor_row.T[:, :, None]).astype(jnp.bfloat16)
    returned = lax.all_to_all(pieces, "head", split_axis=0, concat_axis=1, tiled=True)
    returned = returned.reshape(tok_rows, groups * heads_dev * value_dim)
    gated = jax.nn.sigmoid(out_gate.astype(jnp.float32)) * returned.astype(jnp.float32)
    return gated.astype(jnp.bfloat16)


def solution(mesh):
    return jax.shard_map(
        per_device,
        mesh=mesh,
        in_specs=(
            P(("seq", "head"), None),
            P(("seq", "head"), None),
            P(("seq", "head"), None),
            P("head", "seq"),
            P("head", "seq"),
            P(("seq", "head"), None),
        ),
        out_specs=P(("seq", "head"), None),
        check_vma=False,
    )
```

profile of v0, /device:TPU:486, one launch (start us, length us, event | category | flops | bytes accessed | tf_op | source)
XLA Modules:
  0.0 608.4 jit_solution(11629457740422896061)
XLA Ops:
  6.5 1.7 copy.46
  8.3 4.5 all-to-all-start
  14.9 1.9 copy.44
  16.7 2.0 fusion.16
  18.7 1.5 all-to-all-done
  20.3 3.5 all-to-all-start.1
  23.8 2.0 subtract_exponential_fusion.1
  25.9 8.2 %all-to-all-done.1 = bf16[64,8,512]{2,0,1:T(8,128)(2,1)S(1)} async-done(((bf16[64,8,512]{2,0,1:T(8,128)(2,1)}), bf16[64,8,512]{2,0,1:T(8,128)(2,1)S(1)}, u32[]{:S(2)}, u32[]{:S(2)}) %all-to-all-start.1) | async-done | bytes 524320 | tf_op jit(solution)/shard_map/all_to_all | solution.py:46
  35.3 1.7 copy.45
  37.0 3.4 all-to-all-start.2
  41.7 1.3 bitcast_dynamic-update-slice_fusion
  43.0 1.3 dynamic-update-slice.1
  44.3 139.2 %all-reduce.2 = (f32[64]{0:T(128)S(1)}, f32[64]{0:T(128)S(1)}) all-reduce(f32[64]{0:T(128)S(1)} %bitcast_dynamic-update-slice_fusion, f32[64]{0:T(128)S(1)} %dynamic-update-slice.1), channel_id=1, replica_groups=mesh['seq'=64,'head'=8] {'seq'}, use_global_device_ids=true, to_apply=%add | all-reduce | flops 128 | bytes 1024
  184.6 81.6 %all-gather.2 = f32[64,1,256]{2,1,0:T(1,128)S(1)} all-gather(f32[1,1,256]{2,1,0:T(1,128)S(1)} %bitcast.147), channel_id=3, replica_groups=mesh['seq'=64,'head'=8] {'seq'}, dimensions={0}, use_global_device_ids=true | all-gather | bytes 66560 | tf_op jit(solution)/shard_map/all_gather | solution.py:11
  266.3 57.4 %all-gather.5.cloned.1.call-done = f32[16384,512]{1,0:T(8,128)} async-done(((f32[256,512]{1,0:T(8,128)}), f32[16384,512]{1,0:T(8,128)}) %all-gather.5.cloned.1.call-update) | async-done | bytes 33554448 | tf_op jit(solution)/shard_map/all_gather | solution.py:11
  323.8 254.2 %while.16 = (s32[]{:T(128)}, f32[1,256,512]{2,1,0:T(8,128)S(1)}, f32[1,256]{1,0:T(1,128)S(1)}, f32[1]{0:T(128)}, s32[]{:T(128)}, /*index=5*/f32[64,1]{0,1:T(1,12...) while((s32[]{:T(128)}, f32[1,256,512]{2,1,0:T(8,128)S(1)}, ...), condition=%wide.region_5.6_spmd, body=%wide.region_4.5_spmd.sunk | while | flops 393993 | bytes 1576195 | solution.py:19
  334.6 1.3 bitcast_add_fusion.5
  338.6 1.3 bitcast_add_fusion.5
  342.6 1.3 bitcast_add_fusion.5
  346.7 1.3 bitcast_add_fusion.5
  350.7 1.3 bitcast_add_fusion.5
  358.8 1.3 bitcast_add_fusion.5
  362.8 1.3 bitcast_add_fusion.5
  366.8 1.3 bitcast_add_fusion.5
  370.9 1.3 bitcast_add_fusion.5
  374.9 1.3 bitcast_add_fusion.5
  387.0 1.3 bitcast_add_fusion.5
  391.1 1.3 bitcast_add_fusion.5
  395.1 1.3 bitcast_add_fusion.5
  399.1 1.3 bitcast_add_fusion.5
  411.2 1.3 bitcast_add_fusion.5
  415.3 1.3 bitcast_add_fusion.5
  419.3 1.3 bitcast_add_fusion.5
  423.3 1.3 bitcast_add_fusion.5
  427.4 1.3 bitcast_add_fusion.5
  435.4 1.3 bitcast_add_fusion.5
  439.5 1.3 bitcast_add_fusion.5
  443.5 1.3 bitcast_add_fusion.5
  447.5 1.3 bitcast_add_fusion.5
  451.6 1.3 bitcast_add_fusion.5
  463.7 1.3 bitcast_add_fusion.5
  467.7 1.3 bitcast_add_fusion.5
  471.7 1.3 bitcast_add_fusion.5
  475.8 1.3 bitcast_add_fusion.5
  487.9 1.3 bitcast_add_fusion.5
  491.9 1.3 bitcast_add_fusion.5
  496.0 1.3 bitcast_add_fusion.5
  583.1 14.5 %all_to_all.54 = bf16[8,2,16384]{2,1,0:T(2,128)(2,1)S(1)} all-to-all(bf16[8,2,16384]{2,1,0:T(2,128)(2,1)S(1)} %reshape.499), channel_id=1, replica_groups=mesh['seq'=64,'head'=8] {'head'}, dimensions={0} | all-to-all | bytes 1048576 | tf_op jit(solution)/shard_map/all_to_all | solution.py:100
  (196 shorter events, 98.3 us)
Async XLA Ops:
  6.5 593.9 %copy-start = (bf16[64,4096]{1,0:T(8,128)(2,1)S(1)}, bf16[64,4096]{1,0:T(8,128)(2,1)}, u32[]{:S(2)}) copy-start(bf16[64,4096]{1,0:T(8,128)(2,1)} %param.13) | copy-start | bytes 1572868
  8.3 12.0 %all-to-all-start = ((bf16[64,8,256]{2,0,1:T(8,128)(2,1)}), bf16[64,8,256]{2,0,1:T(8,128)(2,1)S(1)}, u32[]{:S(2)}, u32[]{:S(2)}) async-start(bf16[64,8,256]{2,0,1:T(8,128)(2,1)} %bitcast.110), calls=%async_computation | async-start | bytes 524288 | tf_op jit(solution)/shard_map/all_to_all | solution.py:45
  20.3 13.8 %all-to-all-start.1 = ((bf16[64,8,512]{2,0,1:T(8,128)(2,1)}), bf16[64,8,512]{2,0,1:T(8,128)(2,1)S(1)}, u32[]{:S(2)}, u32[]{:S(2)}) async-start(bf16[64,8,512]{2,0,1:T(8,128)(2,1)} %bitcast.108), calls=%async_computation.1 | async-start | bytes 1048576 | tf_op jit(solution)/shard_map/all_to_all | solution.py:46
  23.8 299.9 %all-gather.5.cloned.1.call-start = ((), (), s32[]{:S(2)}) async-start(), calls=%async_computation.4 | async-start | bytes 34078720 | tf_op jit(solution)/shard_map/all_gather | solution.py:11
  37.0 229.2 %all-to-all-start.2 = ((bf16[64,8,256]{2,0,1:T(8,128)(2,1)}), bf16[64,8,256]{2,0,1:T(8,128)(2,1)S(1)}, u32[]{:S(2)}, u32[]{:S(2)}) async-start(bf16[64,8,256]{2,0,1:T(8,128)(2,1)} %bitcast.109), calls=%async_computation.2 | async-start | bytes 524288 | tf_op jit(solution)/shard_map/all_to_all | solution.py:44
Sparse Core Ops, SparseCore 0:
  35.4 288.2 all-gather.4
where the time goes:
time: 614 us; the launch traced here: 608 us
  blocking collectives  235 us (38%)
  loops' own time  131 us (21%)
  other arithmetic  91.3 us (15%)
  waiting for transfers between devices  67.1 us (11%)
  local copies, waits for them, and re-layouts  54 us (9%)
  between operations  13.6 us (2%)
  starting transfers between devices  11.4 us (2%)
    unnamed x1, blocking collectives  139 us
    another operation x1, loops' own time, prefix(): return lax.fori_loop(0, place, one, state)  131 us
    all_gather x1, blocking collectives, prefix(): gathered = jax.tree.map(lambda a: lax.all_gather(a, axis), part)  81.6 us
    add x63, other arithmetic, merge_states(): scale_one[:, None, None] * memory_one  80.5 us
    all_gather x1, waiting for transfers between devices, prefix(): gathered = jax.tree.map(lambda a: lax.all_gather(a, axis), part)  57.4 us
    dynamic_slice x63, local copies, waits for them, and re-layouts, one(): lax.dynamic_index_in_dim(a, lap, 0, False)  41.2 us
    all_to_all x1, blocking collectives, per_device(): lax.all_to_all(pieces, 'head', split_axis=0, concat_axis=1, tiled=True)  14.5 us
  transfers between devices with their start and end apart: 4, of which 3 were waited for; matrix products, arithmetic and copies ran while one was open for 2% of the time, Pallas kernels for 0%

commit v1 on v0

v1 whole, which is shorter than its diff:
```python
import functools

import jax
import jax.numpy as jnp
from jax import lax
from jax.experimental import pallas as pl
from jax.experimental.pallas import tpu as pltpu
from jax.sharding import PartitionSpec as P

MESH = pl.DeviceIdType.MESH
NEG_FILL = -1e30
MEMBERS = 16
CHUNKS = 2
TILE = 128


def kernel(
    sizes,
    q_ref,
    k_ref,
    v_ref,
    ig_ref,
    fg_ref,
    ret_ref,
    qbuf,
    kbuf,
    vbuf,
    wkt,
    within_col,
    weight_col,
    local_max,
    scores,
    mixing,
    entry_rate,
    local_out,
    hdr,
    hdr_all,
    hdr_total,
    hdr_total_all,
    coef_local,
    coef_full,
    entry,
    coef_total,
    mown,
    mrecv,
    usend,
    urecv,
    isend,
    irecv,
    hid,
    send_sem,
    recv_sem,
    relay_sem,
):
    n_seq, n_head = sizes
    n_group = n_seq // MEMBERS
    tok = q_ref.shape[0]
    rows, key_dim = kbuf.shape
    width = vbuf.shape[2]
    value_dim = width * CHUNKS
    part = key_dim // MEMBERS
    seq = lax.axis_index("seq")
    head = lax.axis_index("head")
    me = lax.rem(seq, MEMBERS)
    group = seq // MEMBERS
    base = group * MEMBERS
    head_row = pl.multiple_of(head * tok, tok)

    K, Q, HDR, HDRT = 0, 1, 2, 3
    V, A, B, C, R = (4 + CHUNKS * i for i in range(5))

    def member(j):
        return base + lax.rem(me + j, MEMBERS)

    def stride(j):
        return lax.rem(seq + MEMBERS * j, n_seq)

    def peer(j):
        return lax.rem(head + j, n_head)

    def put(src, dst, which, device):
        pltpu.make_async_remote_copy(
            src_ref=src,
            dst_ref=dst,
            send_sem=send_sem.at[which],
            recv_sem=recv_sem.at[which],
            device_id=device,
            device_id_type=MESH,
        ).start()

    def arrived(ref, which):
        pltpu.make_async_copy(ref, ref, recv_sem.at[which]).wait()

    def sent(ref, which):
        pltpu.make_async_copy(ref, ref, send_sem.at[which]).wait()

    barrier = pltpu.get_barrier_semaphore()
    for j in range(1, n_head):
        pl.semaphore_signal(barrier, inc=1, device_id=(seq, peer(j)), device_id_type=MESH)
    for j in range(1, MEMBERS):
        pl.semaphore_signal(barrier, inc=1, device_id=(member(j), head), device_id_type=MESH)
    for j in (1, n_group - 1):
        pl.semaphore_signal(barrier, inc=1, device_id=(stride(j), head), device_id_type=MESH)

    def local(src, dst, which):
        pltpu.make_async_copy(src, dst, recv_sem.at[which]).start()

    def key_cols(h):
        return pl.ds(pl.multiple_of(h * key_dim, key_dim), key_dim)

    def value_cols(h, c):
        return pl.ds(pl.multiple_of(h * value_dim + c * width, width), width)

    my_rows = pl.ds(head_row, tok)
    local(k_ref.at[:, key_cols(head)], kbuf.at[my_rows], K)
    for c in range(CHUNKS):
        local(v_ref.at[:, value_cols(head, c)], vbuf.at[c, my_rows], V + c)
    local(q_ref.at[:, key_cols(head)], qbuf.at[my_rows], Q)

    gate = ig_ref[...]
    forget = fg_ref[...]
    log_keep = jnp.minimum(forget, 0.0) - jnp.log1p(jnp.exp(-jnp.abs(forget)))
    lane = lax.broadcasted_iota(jnp.int32, (8, rows), 1)
    within_row = jnp.broadcast_to(log_keep, (8, rows))
    step = 1
    while step < rows:
        within_row = within_row + jnp.where(lane >= step, pltpu.roll(within_row, step, 1), 0.0)
        step *= 2
    within_row = within_row[0:1, :]
    decay = within_row[:, rows - 1 : rows]
    gate_less = gate - within_row

    def gate_tile(i, peak):
        at = pl.ds(pl.multiple_of(i * TILE, TILE), TILE)
        t = lax.broadcasted_iota(jnp.int32, (TILE, rows), 0) + i * TILE
        s = lax.broadcasted_iota(jnp.int32, (TILE, rows), 1)
        col = jnp.sum(jnp.where(s <= t, log_keep, 0.0), axis=1, keepdims=True)
        own_gate = jnp.sum(jnp.where(s == t, gate, 0.0), axis=1, keepdims=True)
        since = decay - col + own_gate
        within_col[at, :] = col
        weight_col[at, :] = since
        local_max[at, :] = col + jnp.max(
            jnp.where(s <= t, gate_less, NEG_FILL), axis=1, keepdims=True
        )
        return jnp.maximum(peak, jnp.max(since, axis=0, keepdims=True))

    peak_own = lax.fori_loop(
        0, rows // TILE, gate_tile, jnp.full((1, 1), -jnp.inf, jnp.float32)
    )
    hdr[...] = jnp.zeros_like(hdr)
    hdr[0:1, :] = jnp.broadcast_to(decay, (1, 128))
    hdr[1:2, :] = jnp.broadcast_to(peak_own, (1, 128))
    hdr_total[...] = jnp.zeros_like(hdr_total)
    hdr_total_all[group] = jnp.zeros(hdr_total.shape, jnp.float32)
    for c in range(CHUNKS):
        urecv[c, group] = jnp.zeros(urecv.shape[2:], urecv.dtype)

    pl.semaphore_wait(barrier, n_head - 1 + MEMBERS - 1 + 2)
    pl.semaphore_signal(relay_sem, inc=1, device_id=(stride(1), head), device_id_type=MESH)

    for j in range(1, n_head):
        h = peer(j)
        put(k_ref.at[:, key_cols(h)], kbuf.at[my_rows], K, (seq, h))
    for c in range(CHUNKS):
        for j in range(1, n_head):
            h = peer(j)
            put(v_ref.at[:, value_cols(h, c)], vbuf.at[c, my_rows], V + c, (seq, h))
    for j in range(1, n_head):
        h = peer(j)
        put(q_ref.at[:, key_cols(h)], qbuf.at[my_rows], Q, (seq, h))

    arrived(kbuf, K)

    def key_tile(i, normal):
        at = pl.ds(pl.multiple_of(i * TILE, TILE), TILE)
        weight = jnp.exp(weight_col[at, :] - peak_own)
        weighted = weight * kbuf[at, :].astype(jnp.float32)
        wkt[:, at] = weighted.T.astype(jnp.bfloat16)
        return normal + jnp.sum(weighted, axis=0, keepdims=True)

    normal_own = lax.fori_loop(
        0, rows // TILE, key_tile, jnp.zeros((1, key_dim), jnp.float32)
    )
    for i in range(key_dim // 128):
        hdr[2 + i : 3 + i, :] = normal_own[:, i * 128 : (i + 1) * 128]
    hdr_all[me] = hdr[...]
    for j in range(1, MEMBERS):
        put(hdr, hdr_all.at[me], HDR, (member(j), head))

    for c in range(CHUNKS):
        arrived(vbuf.at[c], V + c)
        own = jnp.dot(wkt[...], vbuf[c], preferred_element_type=jnp.float32)
        mown[c] = own.astype(jnp.bfloat16).reshape(MEMBERS, part, width)
        for j in range(1, MEMBERS):
            g = lax.rem(me + j, MEMBERS)
            put(mown.at[c, g], mrecv.at[c, me], A + c, (base + g, head))
        mrecv[c, me] = mown[c, me]

    norm_rows = slice(2, 2 + key_dim // 128)
    no_peak = jnp.full((1, 128), NEG_FILL, jnp.float32)
    no_norm = jnp.zeros((key_dim // 128, 128), jnp.float32)

    arrived(hdr_all.at[pl.ds(0, MEMBERS - 1)], HDR)
    peak, norm, total = no_peak, no_norm, jnp.zeros((1, 128), jnp.float32)
    for g in range(MEMBERS):
        d, p = hdr_all[g, 0:1, :], hdr_all[g, 1:2, :]
        new = jnp.maximum(d + peak, p)
        older, newer = jnp.exp(d + peak - new), jnp.exp(p - new)
        coef_local[g, 0:1, :] = older
        coef_local[g, 1:2, :] = newer
        norm = older * norm + newer * hdr_all[g, norm_rows, :]
        peak, total = new, total + d
    hdr_total[0:1, :] = total
    hdr_total[1:2, :] = peak
    hdr_total[norm_rows, :] = norm
    pl.semaphore_wait(relay_sem, 1)
    for j in range(1, n_group):
        put(hdr_total, hdr_total_all.at[group], HDRT, (stride(j), head))

    arrived(qbuf, Q)
    scale = key_dim ** (-0.5)

    def score_tile(i, carry):
        at = pl.ds(pl.multiple_of(i * TILE, TILE), TILE)
        scores[at, :] = lax.dot_general(
            qbuf[at, :], kbuf[...], (((1,), (1,)), ((), ())), preferred_element_type=jnp.float32
        )
        return carry

    lax.fori_loop(0, rows // TILE, score_tile, 0)

    def wide(row):
        return jnp.concatenate([row] * (width // 128), axis=1)

    for c in range(CHUNKS):
        arrived(mrecv.at[c, pl.ds(0, MEMBERS - 1)], A + c)
        state = jnp.zeros((part, width), jnp.float32)
        for g in range(MEMBERS):
            state = (
                wide(coef_local[g, 0:1, :]) * state
                + wide(coef_local[g, 1:2, :]) * mrecv[c, g].astype(jnp.float32)
            )
        usend[c] = state.astype(jnp.bfloat16)
        for j in range(1, n_group):
            put(usend.at[c], urecv.at[c, group], B + c, (stride(j), head))

    arrived(hdr_total_all.at[pl.ds(0, n_group - 1)], HDRT)
    peak, norm = no_peak, no_norm
    for j in range(n_group - 1):
        d, p = hdr_total_all[j, 0:1, :], hdr_total_all[j, 1:2, :]
        new = jnp.maximum(d + peak, p)
        used = j < group
        older = jnp.where(used, jnp.exp(d + peak - new), 1.0)
        newer = jnp.where(used, jnp.exp(p - new), 0.0)
        coef_total[j, 0:1, :] = older
        coef_total[j, 1:2, :] = newer
        norm = jnp.where(used, older * norm + newer * hdr_total_all[j, norm_rows, :], norm)
        peak = jnp.where(used, new, peak)
    for g in range(MEMBERS):
        entry[g, 1:2, :] = peak
        entry[g, norm_rows, :] = norm
        d, p = hdr_all[g, 0:1, :], hdr_all[g, 1:2, :]
        new = jnp.maximum(d + peak, p)
        older, newer = jnp.exp(d + peak - new), jnp.exp(p - new)
        coef_full[g, 0:1, :] = older
        coef_full[g, 1:2, :] = newer
        norm = older * norm + newer * hdr_all[g, norm_rows, :]
        peak = new

    my_entry = entry[me]
    peak_in = my_entry[1:2, 0:1]
    normal_in = jnp.concatenate(
        [my_entry[2 + i : 3 + i, :] for i in range(key_dim // 128)], axis=1
    )

    def mixing_tile(i, carry):
        at = pl.ds(pl.multiple_of(i * TILE, TILE), TILE)
        t = lax.broadcasted_iota(jnp.int32, (TILE, rows), 0) + i * TILE
        s = lax.broadcasted_iota(jnp.int32, (TILE, rows), 1)
        col = within_col[at, :]
        entry_log = col + peak_in
        peak_row = jnp.maximum(entry_log, local_max[at, :])
        logs = jnp.where(s <= t, (col - peak_row) + gate_less, NEG_FILL)
        mix = jnp.exp(logs) * (scores[at, :] * scale)
        mixing[at, :] = mix.astype(jnp.bfloat16)
        rate = jnp.exp(entry_log - peak_row)
        from_normal = jnp.sum(
            qbuf[at, :].astype(jnp.float32) * normal_in, axis=1, keepdims=True
        )
        below = jnp.sum(mix, axis=1, keepdims=True) + rate * (from_normal * scale)
        inverse = 1.0 / jnp.maximum(jnp.abs(below), 1.0)
        entry_rate[at, 0:1] = rate * inverse * scale
        entry_rate[at, 1:2] = inverse
        return carry

    lax.fori_loop(0, rows // TILE, mixing_tile, 0)

    for c in range(CHUNKS):
        arrived(urecv.at[c, pl.ds(0, n_group - 1)], B + c)
        state = jnp.zeros((part, width), jnp.float32)
        for j in range(n_group - 1):
            state = jnp.where(
                j < group,
                wide(coef_total[j, 0:1, :]) * state
                + wide(coef_total[j, 1:2, :]) * urecv[c, j].astype(jnp.float32),
                state,
            )
        for g in range(MEMBERS):
            isend[c, g] = state.astype(jnp.bfloat16)
            state = (
                wide(coef_full[g, 0:1, :]) * state
                + wide(coef_full[g, 1:2, :]) * mrecv[c, g].astype(jnp.float32)
            )
        my_part = pl.ds(pl.multiple_of(me * part, part), part)
        for j in range(1, MEMBERS):
            g = lax.rem(me + j, MEMBERS)
            put(isend.at[c, g], irecv.at[c, my_part], C + c, (base + g, head))
        irecv[c, my_part] = isend[c, me]

    def local_tile(i, carry):
        at = pl.ds(pl.multiple_of(i * TILE, TILE), TILE)
        for c in range(CHUNKS):
            local_out[c, at, :] = entry_rate[at, 1:2] * jnp.dot(
                mixing[at, :], vbuf[c], preferred_element_type=jnp.float32
            )
        return carry

    lax.fori_loop(0, rows // TILE, local_tile, 0)

    for c in range(CHUNKS):
        arrived(irecv.at[c, pl.ds(0, key_dim - part)], C + c)

        def out_tile(i, carry):
            at = pl.ds(pl.multiple_of(i * TILE, TILE), TILE)
            from_memory = jnp.dot(
                qbuf[at, :], irecv[c], preferred_element_type=jnp.float32
            )
            hid[c, at, :] = (
                local_out[c, at, :] + entry_rate[at, 0:1] * from_memory
            ).astype(jnp.bfloat16)
            return carry

        lax.fori_loop(0, rows // TILE, out_tile, 0)
        for j in range(1, n_head):
            h = peer(j)
            put(
                hid.at[c, pl.ds(pl.multiple_of(h * tok, tok), tok)],
                ret_ref.at[:, value_cols(head, c)],
                R + c,
                (seq, h),
            )
        local(hid.at[c, my_rows], ret_ref.at[:, value_cols(head, c)], R + c)

    for c in range(CHUNKS):
        arrived(hid.at[c], R + c)

    peers_rows = pl.ds(0, rows - tok)
    sent(kbuf.at[peers_rows], K)
    sent(qbuf.at[peers_rows], Q)
    sent(hdr_all.at[pl.ds(0, MEMBERS - 1)], HDR)
    sent(hdr_total_all.at[pl.ds(0, n_group - 1)], HDRT)
    for c in range(CHUNKS):
        sent(vbuf.at[c, peers_rows], V + c)
        sent(mrecv.at[c, pl.ds(0, MEMBERS - 1)], A + c)
        sent(urecv.at[c, pl.ds(0, n_group - 1)], B + c)
        sent(irecv.at[c, pl.ds(0, key_dim - part)], C + c)
        sent(hid.at[c, peers_rows], R + c)


def per_device(n_seq, n_head, queries, keys, values, in_gate, forget_gate, out_gate):
    tok = queries.shape[0]
    rows = tok * n_head
    key_dim = queries.shape[1] // n_head
    value_dim = values.shape[1] // n_head
    width = value_dim // CHUNKS
    part = key_dim // MEMBERS
    n_group = n_seq // MEMBERS
    bf16, f32 = jnp.bfloat16, jnp.float32
    scratch = [
        pltpu.VMEM((rows, key_dim), bf16),
        pltpu.VMEM((rows, key_dim), bf16),
        pltpu.VMEM((CHUNKS, rows, width), bf16),
        pltpu.VMEM((key_dim, rows), bf16),
        pltpu.VMEM((rows, 1), f32),
        pltpu.VMEM((rows, 1), f32),
        pltpu.VMEM((rows, 1), f32),
        pltpu.VMEM((rows, rows), f32),
        pltpu.VMEM((rows, rows), bf16),
        pltpu.VMEM((rows, 2), f32),
        pltpu.VMEM((CHUNKS, rows, width), f32),
        pltpu.VMEM((8, 128), f32),
        pltpu.VMEM((MEMBERS, 8, 128), f32),
        pltpu.VMEM((8, 128), f32),
        pltpu.VMEM((n_group, 8, 128), f32),
        pltpu.VMEM((MEMBERS, 8, 128), f32),
        pltpu.VMEM((MEMBERS, 8, 128), f32),
        pltpu.VMEM((MEMBERS, 8, 128), f32),
        pltpu.VMEM((n_group, 8, 128), f32),
        pltpu.VMEM((CHUNKS, MEMBERS, part, width), bf16),
        pltpu.VMEM((CHUNKS, MEMBERS, part, width), bf16),
        pltpu.VMEM((CHUNKS, part, width), bf16),
        pltpu.VMEM((CHUNKS, n_group, part, width), bf16),
        pltpu.VMEM((CHUNKS, MEMBERS, part, width), bf16),
        pltpu.VMEM((CHUNKS, key_dim, width), bf16),
        pltpu.VMEM((CHUNKS, rows, width), bf16),
        pltpu.SemaphoreType.DMA((4 + 5 * CHUNKS,)),
        pltpu.SemaphoreType.DMA((4 + 5 * CHUNKS,)),
        pltpu.SemaphoreType.REGULAR,
    ]
    anywhere = pl.BlockSpec(memory_space=pl.ANY)
    vmem = pl.BlockSpec(memory_space=pltpu.VMEM)
    returned = pl.pallas_call(
        functools.partial(kernel, (n_seq, n_head)),
        out_shape=jax.ShapeDtypeStruct((tok, n_head * value_dim), bf16),
        in_specs=[anywhere, anywhere, anywhere, vmem, vmem],
        out_specs=anywhere,
        scratch_shapes=scratch,
        compiler_params=pltpu.CompilerParams(
            collective_id=0, has_side_effects=True, vmem_limit_bytes=40 * 2**20
        ),
    )(queries, keys, values, in_gate, forget_gate)
    gated = jax.nn.sigmoid(out_gate.astype(f32)) * returned.astype(f32)
    return gated.astype(bf16)


def solution(mesh):
    return jax.shard_map(
        functools.partial(per_device, mesh.shape["seq"], mesh.shape["head"]),
        mesh=mesh,
        in_specs=(
            P(("seq", "head"), None),
            P(("seq", "head"), None),
            P(("seq", "head"), None),
            P("head", "seq"),
            P("head", "seq"),
            P(("seq", "head"), None),
        ),
        out_specs=P(("seq", "head"), None),
        check_vma=False,
    )
```

time: 614 us -> 57.2 us (0.09)
  the two profiles are of different devices: /device:TPU:486 before, /device:TPU:1 now
where the time goes in v1:
time: 57.2 us; the launch traced here: 56.9 us
  Pallas kernels  51.5 us (90%)
  local copies, waits for them, and re-layouts  4.31 us (8%)
  other arithmetic  1.07 us (2%)
    pallas_call x1, Pallas kernels, per_device(): pl.pallas_call(functools.partial(kernel, (n_seq, n_head)), out_shape=jax....  51.5 us
    unnamed x12, local copies, waits for them, and re-layouts  4.31 us

profile of v1, /device:TPU:1, one launch (start us, length us, event | category | flops | bytes accessed | tf_op | source)
XLA Modules:
  0.0 56.9 jit_solution(10741581002283773849)
XLA Ops:
  0.0 0.0 copy-start
  0.0 1.0 %copy-done = bf16[64,4096]{1,0:T(8,128)(2,1)S(1)} copy-done((bf16[64,4096]{1,0:T(8,128)(2,1)S(1)}, bf16[64,4096]{1,0:T(8,128)(2,1)}, u32[]{:S(2)}) %copy-start) | copy-done | bytes 524312
  1.0 0.0 copy-start.1
  1.0 0.9 %copy-done.1 = bf16[64,2048]{1,0:T(8,128)(2,1)S(1)} copy-done((bf16[64,2048]{1,0:T(8,128)(2,1)S(1)}, bf16[64,2048]{1,0:T(8,128)(2,1)}, u32[]{:S(2)}) %copy-start.1) | copy-done | bytes 262168
  2.0 0.0 copy-start.2
  2.0 0.9 %copy-done.2 = bf16[64,2048]{1,0:T(8,128)(2,1)S(1)} copy-done((bf16[64,2048]{1,0:T(8,128)(2,1)S(1)}, bf16[64,2048]{1,0:T(8,128)(2,1)}, u32[]{:S(2)}) %copy-start.2) | copy-done | bytes 262168
  2.9 0.0 copy-start.3
  2.9 0.7 %copy-done.3 = f32[1,512]{1,0:T(1,128)S(1)} copy-done((f32[1,512]{1,0:T(1,128)S(1)}, f32[1,512]{1,0:T(1,128)}, u32[]{:S(2)}) %copy-start.3) | copy-done | bytes 2072
  3.6 0.0 copy-start.4
  3.6 0.7 %copy-done.4 = f32[1,512]{1,0:T(1,128)S(1)} copy-done((f32[1,512]{1,0:T(1,128)S(1)}, f32[1,512]{1,0:T(1,128)}, u32[]{:S(2)}) %copy-start.4) | copy-done | bytes 2072
  4.3 0.0 copy-start.5
  4.3 51.5 %shard_map.64 = bf16[64,4096]{1,0:T(8,128)(2,1)S(1)} custom-call(bf16[64,2048]{1,0:T(8,128)(2,1)S(1)} %copy-done.1, bf16[64,2048]{1,0:T(8,128)(2,1)S(1)} %copy-done.2, bf16[64,4096]{1,0:T(8,128)(2,1)S(1)} %copy-done, f32[1,512]{1,0:T(1,128)S(1)} %copy-done.3, f32[1,512]{1,0:T(1,128)S(1)} %copy-done.4), custom_call_target="tpu_custom_call" | custom-call | tf_op jit(solution)/shard_map/pallas_call | solution.py:412
  55.9 0.0 copy-done.5
  55.9 1.1 %multiply_convert_fusion = bf16[64,4096]{1,0:T(8,128)(2,1)} fusion(bf16[64,4096]{1,0:T(8,128)(2,1)S(1)} %shard_map.64, bf16[64,4096]{1,0:T(8,128)(2,1)S(1)} %copy-done.5), kind=kLoop, calls=%fused_computation | loop fusion | flops 1835008 | bytes 1572864 | tf_op jit(solution)/shard_map/convert_element_type | solution.py:423
Async XLA Ops:
  0.0 1.0 %copy-start = (bf16[64,4096]{1,0:T(8,128)(2,1)S(1)}, bf16[64,4096]{1,0:T(8,128)(2,1)}, u32[]{:S(2)}) copy-start(bf16[64,4096]{1,0:T(8,128)(2,1)} %v_ref.1) | copy-start | bytes 1572868
  1.0 0.9 %copy-start.1 = (bf16[64,2048]{1,0:T(8,128)(2,1)S(1)}, bf16[64,2048]{1,0:T(8,128)(2,1)}, u32[]{:S(2)}) copy-start(bf16[64,2048]{1,0:T(8,128)(2,1)} %q_ref.1) | copy-start | bytes 786436
  2.0 0.9 %copy-start.2 = (bf16[64,2048]{1,0:T(8,128)(2,1)S(1)}, bf16[64,2048]{1,0:T(8,128)(2,1)}, u32[]{:S(2)}) copy-start(bf16[64,2048]{1,0:T(8,128)(2,1)} %k_ref.1) | copy-start | bytes 786436
  2.9 0.7 %copy-start.3 = (f32[1,512]{1,0:T(1,128)S(1)}, f32[1,512]{1,0:T(1,128)}, u32[]{:S(2)}) copy-start(f32[1,512]{1,0:T(1,128)} %ig_ref.1) | copy-start | bytes 6148
  3.6 0.7 %copy-start.4 = (f32[1,512]{1,0:T(1,128)S(1)}, f32[1,512]{1,0:T(1,128)}, u32[]{:S(2)}) copy-start(f32[1,512]{1,0:T(1,128)} %fg_ref.1) | copy-start | bytes 6148
  4.3 51.6 %copy-start.5 = (bf16[64,4096]{1,0:T(8,128)(2,1)S(1)}, bf16[64,4096]{1,0:T(8,128)(2,1)}, u32[]{:S(2)}) copy-start(bf16[64,4096]{1,0:T(8,128)(2,1)} %param.11) | copy-start | bytes 1572868

commit v2 on v1

--- a/solution.py
+++ b/solution.py
@@ -22,6 +22,7 @@
     ig_ref,
     fg_ref,
     ret_ref,
+    gates,
     qbuf,
     kbuf,
     vbuf,
@@ -66,24 +67,32 @@
     base = group * MEMBERS
     head_row = pl.multiple_of(head * tok, tok)
 
-    K, Q, HDR, HDRT = 0, 1, 2, 3
-    V, A, B, C, R = (4 + CHUNKS * i for i in range(5))
+    later = n_group - 1
+    K, Q, HDR, GATE = 0, 1, 2, 3
+    V, A, C, R = (4 + CHUNKS * i for i in range(4))
+    HDRT = 4 + 4 * CHUNKS
+    B = HDRT + later
 
     def member(j):
         return base + lax.rem(me + j, MEMBERS)
 
-    def stride(j):
-        return lax.rem(seq + MEMBERS * j, n_seq)
+    def each_later(act):
+        for j in range(1, n_group):
+            pl.when(group + j < n_group)(functools.partial(act, j, seq + MEMBERS * j))
+
+    def each_earlier(act):
+        for j in range(later):
+            pl.when(j < group)(functools.partial(act, j, j * MEMBERS + me))
 
     def peer(j):
         return lax.rem(head + j, n_head)
 
-    def put(src, dst, which, device):
+    def put(src, dst, which, device, lands=None):
         pltpu.make_async_remote_copy(
             src_ref=src,
             dst_ref=dst,
             send_sem=send_sem.at[which],
-            recv_sem=recv_sem.at[which],
+            recv_sem=recv_sem.at[which if lands is None else lands],
             device_id=device,
             device_id_type=MESH,
         ).start()
@@ -93,17 +102,23 @@
 
     def sent(ref, which):
         pltpu.make_async_copy(ref, ref, send_sem.at[which]).wait()
+
+    def local(src, dst, which):
+        pltpu.make_async_copy(src, dst, recv_sem.at[which]).start()
+
+    local(ig_ref, gates.at[0], GATE)
+    local(fg_ref, gates.at[1], GATE)
 
     barrier = pltpu.get_barrier_semaphore()
     for j in range(1, n_head):
         pl.semaphore_signal(barrier, inc=1, device_id=(seq, peer(j)), device_id_type=MESH)
     for j in range(1, MEMBERS):
         pl.semaphore_signal(barrier, inc=1, device_id=(member(j), head), device_id_type=MESH)
-    for j in (1, n_group - 1):
-        pl.semaphore_signal(barrier, inc=1, device_id=(stride(j), head), device_id_type=MESH)
-
-    def local(src, dst, which):
-        pltpu.make_async_copy(src, dst, recv_sem.at[which]).start()
+
+    def greet(j, there):
+        pl.semaphore_signal(barrier, inc=1, device_id=(there, head), device_id_type=MESH)
+
+    each_later(greet)
 
     def key_cols(h):
         return pl.ds(pl.multiple_of(h * key_dim, key_dim), key_dim)
@@ -117,8 +132,9 @@
         local(v_ref.at[:, value_cols(head, c)], vbuf.at[c, my_rows], V + c)
     local(q_ref.at[:, key_cols(head)], qbuf.at[my_rows], Q)
 
-    gate = ig_ref[...]
-    forget = fg_ref[...]
+    arrived(gates, GATE)
+    gate = gates[0]
+    forget = gates[1]
     log_keep = jnp.minimum(forget, 0.0) - jnp.log1p(jnp.exp(-jnp.abs(forget)))
     lane = lax.broadcasted_iota(jnp.int32, (8, rows), 1)
     within_row = jnp.broadcast_to(log_keep, (8, rows))
@@ -151,12 +167,20 @@
     hdr[0:1, :] = jnp.broadcast_to(decay, (1, 128))
     hdr[1:2, :] = jnp.broadcast_to(peak_own, (1, 128))
     hdr_total[...] = jnp.zeros_like(hdr_total)
-    hdr_total_all[group] = jnp.zeros(hdr_total.shape, jnp.float32)
-    for c in range(CHUNKS):
-        urecv[c, group] = jnp.zeros(urecv.shape[2:], urecv.dtype)
-
-    pl.semaphore_wait(barrier, n_head - 1 + MEMBERS - 1 + 2)
-    pl.semaphore_signal(relay_sem, inc=1, device_id=(stride(1), head), device_id_type=MESH)
+    for j in range(later):
+
+        @pl.when(j >= group)
+        def _():
+            hdr_total_all[j] = jnp.zeros(hdr_total.shape, jnp.float32)
+            for c in range(CHUNKS):
+                urecv[c, j] = jnp.zeros(urecv.shape[2:], urecv.dtype)
+
+    pl.semaphore_wait(barrier, n_head - 1 + MEMBERS - 1 + group)
+
+    def answer(j, there):
+        pl.semaphore_signal(relay_sem, inc=1, device_id=(there, head), device_id_type=MESH)
+
+    each_earlier(answer)
 
     for j in range(1, n_head):
         h = peer(j)
@@ -213,9 +237,15 @@
     hdr_total[0:1, :] = total
     hdr_total[1:2, :] = peak
     hdr_total[norm_rows, :] = norm
-    pl.semaphore_wait(relay_sem, 1)
-    for j in range(1, n_group):
-        put(hdr_total, hdr_total_all.at[group], HDRT, (stride(j), head))
+
+    @pl.when(group < later)
+    def _():
+        pl.semaphore_wait(relay_sem, later - group)
+
+    def send_header(j, there):
+        put(hdr_total, hdr_total_all.at[group], HDRT + j - 1, (there, head), HDRT + group)
+
+    each_later(send_header)
 
     arrived(qbuf, Q)
     scale = key_dim ** (-0.5)
@@ -241,10 +271,14 @@
                 + wide(coef_local[g, 1:2, :]) * mrecv[c, g].astype(jnp.float32)
             )
         usend[c] = state.astype(jnp.bfloat16)
-        for j in range(1, n_group):
-            put(usend.at[c], urecv.at[c, group], B + c, (stride(j), head))
-
-    arrived(hdr_total_all.at[pl.ds(0, n_group - 1)], HDRT)
+
+        def send_total(j, there):
+            at = B + later * c
+            put(usend.at[c], urecv.at[c, group], at + j - 1, (there, head), at + group)
+
+        each_later(send_total)
+
+    each_earlier(lambda j, there: arrived(hdr_total_all.at[j], HDRT + j))
     peak, norm = no_peak, no_norm
     for j in range(n_group - 1):
         d, p = hdr_total_all[j, 0:1, :], hdr_total_all[j, 1:2, :]
@@ -296,7 +330,7 @@
     lax.fori_loop(0, rows // TILE, mixing_tile, 0)
 
     for c in range(CHUNKS):
-        arrived(urecv.at[c, pl.ds(0, n_group - 1)], B + c)
+        each_earlier(lambda j, there: arrived(urecv.at[c, j], B + later * c + j))
         state = jnp.zeros((part, width), jnp.float32)
         for j in range(n_group - 1):
             state = jnp.where(
@@ -358,11 +392,11 @@
     sent(kbuf.at[peers_rows], K)
     sent(qbuf.at[peers_rows], Q)
     sent(hdr_all.at[pl.ds(0, MEMBERS - 1)], HDR)
-    sent(hdr_total_all.at[pl.ds(0, n_group - 1)], HDRT)
+    each_later(lambda j, there: sent(hdr_total, HDRT + j - 1))
     for c in range(CHUNKS):
         sent(vbuf.at[c, peers_rows], V + c)
         sent(mrecv.at[c, pl.ds(0, MEMBERS - 1)], A + c)
-        sent(urecv.at[c, pl.ds(0, n_group - 1)], B + c)
+        each_later(lambda j, there: sent(usend.at[c], B + later * c + j - 1))
         sent(irecv.at[c, pl.ds(0, key_dim - part)], C + c)
         sent(hid.at[c, peers_rows], R + c)
 
@@ -376,7 +410,9 @@
     part = key_dim // MEMBERS
     n_group = n_seq // MEMBERS
     bf16, f32 = jnp.bfloat16, jnp.float32
+    n_sem = 4 + 4 * CHUNKS + (n_group - 1) * (1 + CHUNKS)
     scratch = [
+        pltpu.VMEM((2, 1, rows), f32),
         pltpu.VMEM((rows, key_dim), bf16),
         pltpu.VMEM((rows, key_dim), bf16),
         pltpu.VMEM((CHUNKS, rows, width), bf16),
@@ -403,20 +439,20 @@
         pltpu.VMEM((CHUNKS, MEMBERS, part, width), bf16),
         pltpu.VMEM((CHUNKS, key_dim, width), bf16),
         pltpu.VMEM((CHUNKS, rows, width), bf16),
-        pltpu.SemaphoreType.DMA((4 + 5 * CHUNKS,)),
-        pltpu.SemaphoreType.DMA((4 + 5 * CHUNKS,)),
+        pltpu.SemaphoreType.DMA((n_sem,)),
+        pltpu.SemaphoreType.DMA((n_sem,)),
         pltpu.SemaphoreType.REGULAR,
     ]
     anywhere = pl.BlockSpec(memory_space=pl.ANY)
-    vmem = pl.BlockSpec(memory_space=pltpu.VMEM)
+    hbm = pl.BlockSpec(memory_space=pltpu.HBM)
     returned = pl.pallas_call(
         functools.partial(kernel, (n_seq, n_head)),
-        out_shape=jax.ShapeDtypeStruct((tok, n_head * value_dim), bf16),
-        in_specs=[anywhere, anywhere, anywhere, vmem, vmem],
-        out_specs=anywhere,
+        out_shape=pltpu.VMEM((tok, n_head * value_dim), bf16),
+        in_specs=[hbm] * 5,
+        out_specs=pl.BlockSpec(memory_space=pltpu.VMEM),
         scratch_shapes=scratch,
         compiler_params=pltpu.CompilerParams(
-            collective_id=0, has_side_effects=True, vmem_limit_bytes=40 * 2**20
+            collective_id=0, has_side_effects=True, vmem_limit_bytes=60 * 2**20
         ),
     )(queries, keys, values, in_gate, forget_gate)
     gated = jax.nn.sigmoid(out_gate.astype(f32)) * returned.astype(f32)

time: 57.2 us -> 45.4 us (0.79)
  the two profiles are of different devices: /device:TPU:1 before, /device:TPU:129 now
where the time goes in v2:
time: 45.4 us; the launch traced here: 45.3 us
  Pallas kernels  44.2 us (97%)
  other arithmetic  1.07 us (2%)
    pallas_call x1, Pallas kernels, per_device(): pl.pallas_call(functools.partial(kernel, (n_seq, n_head)), out_shape=pltp...  44.2 us
    convert_element_type x1, other arithmetic, per_device(): return gated.astype(bf16)  1.07 us

profile of v2, /device:TPU:129, one launch (start us, length us, event | category | flops | bytes accessed | tf_op | source)
XLA Modules:
  0.0 45.3 jit_solution(16317600544558185684)
XLA Ops:
  0.0 0.0 copy-start
  0.0 44.2 %shard_map.64 = bf16[64,4096]{1,0:T(8,128)(2,1)S(1)} custom-call(bf16[64,2048]{1,0:T(8,128)(2,1)} %q_ref.1, bf16[64,2048]{1,0:T(8,128)(2,1)} %k_ref.1, bf16[64,4096]{1,0:T(8,128)(2,1)} %v_ref.1, f32[1,512]{1,0:T(1,128)} %ig_ref.1, f32[1,512]{1,0:T(1,128)} %fg_ref.1), custom_call_target="tpu_custom_call" | custom-call | tf_op jit(solution)/shard_map/pallas_call | solution.py:448
  44.2 0.0 copy-done
  44.2 1.1 %multiply_convert_fusion = bf16[64,4096]{1,0:T(8,128)(2,1)} fusion(bf16[64,4096]{1,0:T(8,128)(2,1)S(1)} %shard_map.64, bf16[64,4096]{1,0:T(8,128)(2,1)S(1)} %copy-done), kind=kLoop, calls=%fused_computation | loop fusion | flops 1835008 | bytes 1572864 | tf_op jit(solution)/shard_map/convert_element_type | solution.py:459
Async XLA Ops:
  0.0 44.2 %copy-start = (bf16[64,4096]{1,0:T(8,128)(2,1)S(1)}, bf16[64,4096]{1,0:T(8,128)(2,1)}, u32[]{:S(2)}) copy-start(bf16[64,4096]{1,0:T(8,128)(2,1)} %param.11) | copy-start | bytes 1572868

commit v3 on v2

--- a/solution.py
+++ b/solution.py
@@ -10,8 +10,9 @@
 MESH = pl.DeviceIdType.MESH
 NEG_FILL = -1e30
 MEMBERS = 16
-CHUNKS = 2
+CHUNKS = 4
 TILE = 128
+PEERS = ((2, 0), (1, 0), (3, 0), (2, 1), (1, 1), (3, 1), (0, 1))
 
 
 def kernel(
@@ -77,7 +78,7 @@
         return base + lax.rem(me + j, MEMBERS)
 
     def each_later(act):
-        for j in range(1, n_group):
+        for j in (2, 3, 1):
             pl.when(group + j < n_group)(functools.partial(act, j, seq + MEMBERS * j))
 
     def each_earlier(act):
@@ -85,7 +86,10 @@
             pl.when(j < group)(functools.partial(act, j, j * MEMBERS + me))
 
     def peer(j):
-        return lax.rem(head + j, n_head)
+        chip, flip = PEERS[j - 1]
+        core = lax.rem(head, 2)
+        there = lax.rem(head // 2 + chip, n_head // 2)
+        return 2 * there + (1 - core if flip else core)
 
     def put(src, dst, which, device, lands=None):
         pltpu.make_async_remote_copy(
@@ -131,6 +135,32 @@
     for c in range(CHUNKS):
         local(v_ref.at[:, value_cols(head, c)], vbuf.at[c, my_rows], V + c)
     local(q_ref.at[:, key_cols(head)], qbuf.at[my_rows], Q)
+
+    for j in range(later):
+
+        @pl.when(j >= group)
+        def _():
+            hdr_total_all[j] = jnp.zeros(hdr_total.shape, jnp.float32)
+            for c in range(CHUNKS):
+                urecv[c, j] = jnp.zeros(urecv.shape[2:], urecv.dtype)
+
+    pl.semaphore_wait(barrier, n_head - 1 + MEMBERS - 1 + group)
+
+    def answer(j, there):
+        pl.semaphore_signal(relay_sem, inc=1, device_id=(there, head), device_id_type=MESH)
+
+    each_earlier(answer)
+
+    for j in range(1, n_head):
+        h = peer(j)
+        put(k_ref.at[:, key_cols(h)], kbuf.at[my_rows], K, (seq, h))
+    for c in range(CHUNKS):
+        for j in range(1, n_head):
+            h = peer(j)
+            put(v_ref.at[:, value_cols(h, c)], vbuf.at[c, my_rows], V + c, (seq, h))
+    for j in range(1, n_head):
+        h = peer(j)
+        put(q_ref.at[:, key_cols(h)], qbuf.at[my_rows], Q, (seq, h))
 
     arrived(gates, GATE)
     gate = gates[0]
@@ -167,32 +197,6 @@
     hdr[0:1, :] = jnp.broadcast_to(decay, (1, 128))
     hdr[1:2, :] = jnp.broadcast_to(peak_own, (1, 128))
     hdr_total[...] = jnp.zeros_like(hdr_total)
-    for j in range(later):
-
-        @pl.when(j >= group)
-        def _():
-            hdr_total_all[j] = jnp.zeros(hdr_total.shape, jnp.float32)
-            for c in range(CHUNKS):
-                urecv[c, j] = jnp.zeros(urecv.shape[2:], urecv.dtype)
-
-    pl.semaphore_wait(barrier, n_head - 1 + MEMBERS - 1 + group)
-
-    def answer(j, there):
-        pl.semaphore_signal(relay_sem, inc=1, device_id=(there, head), device_id_type=MESH)
-
-    each_earlier(answer)
-
-    for j in range(1, n_head):
-        h = peer(j)
-        put(k_ref.at[:, key_cols(h)], kbuf.at[my_rows], K, (seq, h))
-    for c in range(CHUNKS):
-        for j in range(1, n_head):
-            h = peer(j)
-            put(v_ref.at[:, value_cols(h, c)], vbuf.at[c, my_rows], V + c, (seq, h))
-    for j in range(1, n_head):
-        h = peer(j)
-        put(q_ref.at[:, key_cols(h)], qbuf.at[my_rows], Q, (seq, h))
-
     arrived(kbuf, K)
 
     def key_tile(i, normal):
@@ -301,34 +305,6 @@
         norm = older * norm + newer * hdr_all[g, norm_rows, :]
         peak = new
 
-    my_entry = entry[me]
-    peak_in = my_entry[1:2, 0:1]
-    normal_in = jnp.concatenate(
-        [my_entry[2 + i : 3 + i, :] for i in range(key_dim // 128)], axis=1
-    )
-
-    def mixing_tile(i, carry):
-        at = pl.ds(pl.multiple_of(i * TILE, TILE), TILE)
-        t = lax.broadcasted_iota(jnp.int32, (TILE, rows), 0) + i * TILE
-        s = lax.broadcasted_iota(jnp.int32, (TILE, rows), 1)
-        col = within_col[at, :]
-        entry_log = col + peak_in
-        peak_row = jnp.maximum(entry_log, local_max[at, :])
-        logs = jnp.where(s <= t, (col - peak_row) + gate_less, NEG_FILL)
-        mix = jnp.exp(logs) * (scores[at, :] * scale)
-        mixing[at, :] = mix.astype(jnp.bfloat16)
-        rate = jnp.exp(entry_log - peak_row)
-        from_normal = jnp.sum(
-            qbuf[at, :].astype(jnp.float32) * normal_in, axis=1, keepdims=True
-        )
-        below = jnp.sum(mix, axis=1, keepdims=True) + rate * (from_normal * scale)
-        inverse = 1.0 / jnp.maximum(jnp.abs(below), 1.0)
-        entry_rate[at, 0:1] = rate * inverse * scale
-        entry_rate[at, 1:2] = inverse
-        return carry
-
-    lax.fori_loop(0, rows // TILE, mixing_tile, 0)
-
     for c in range(CHUNKS):
         each_earlier(lambda j, there: arrived(urecv.at[c, j], B + later * c + j))
         state = jnp.zeros((part, width), jnp.float32)
@@ -351,6 +327,34 @@
             put(isend.at[c, g], irecv.at[c, my_part], C + c, (base + g, head))
         irecv[c, my_part] = isend[c, me]
 
+    my_entry = entry[me]
+    peak_in = my_entry[1:2, 0:1]
+    normal_in = jnp.concatenate(
+        [my_entry[2 + i : 3 + i, :] for i in range(key_dim // 128)], axis=1
+    )
+
+    def mixing_tile(i, carry):
+        at = pl.ds(pl.multiple_of(i * TILE, TILE), TILE)
+        t = lax.broadcasted_iota(jnp.int32, (TILE, rows), 0) + i * TILE
+        s = lax.broadcasted_iota(jnp.int32, (TILE, rows), 1)
+        col = within_col[at, :]
+        entry_log = col + peak_in
+        peak_row = jnp.maximum(entry_log, local_max[at, :])
+        logs = jnp.where(s <= t, (col - peak_row) + gate_less, NEG_FILL)
+        mix = jnp.exp(logs) * (scores[at, :] * scale)
+        mixing[at, :] = mix.astype(jnp.bfloat16)
+        rate = jnp.exp(entry_log - peak_row)
+        from_normal = jnp.sum(
+            qbuf[at, :].astype(jnp.float32) * normal_in, axis=1, keepdims=True
+        )
+        below = jnp.sum(mix, axis=1, keepdims=True) + rate * (from_normal * scale)
+        inverse = 1.0 / jnp.maximum(jnp.abs(below), 1.0)
+        entry_rate[at, 0:1] = rate * inverse * scale
+        entry_rate[at, 1:2] = inverse
+        return carry
+
+    lax.fori_loop(0, rows // TILE, mixing_tile, 0)
+
     def local_tile(i, carry):
         at = pl.ds(pl.multiple_of(i * TILE, TILE), TILE)
         for c in range(CHUNKS):
@@ -361,28 +365,29 @@
 
     lax.fori_loop(0, rows // TILE, local_tile, 0)
 
+    def send_hidden(c, h):
+        put(
+            hid.at[c, pl.ds(pl.multiple_of(h * tok, tok), tok)],
+            ret_ref.at[:, value_cols(head, c)],
+            R + c,
+            (seq, h),
+        )
+
     for c in range(CHUNKS):
         arrived(irecv.at[c, pl.ds(0, key_dim - part)], C + c)
 
-        def out_tile(i, carry):
-            at = pl.ds(pl.multiple_of(i * TILE, TILE), TILE)
+        for i in range(n_head // 2 - 1, -1, -1):
+            chip = lax.rem(head // 2 + (i + 1) % (n_head // 2), n_head // 2)
+            at = pl.ds(pl.multiple_of(chip * 2 * tok, 2 * tok), 2 * tok)
             from_memory = jnp.dot(
                 qbuf[at, :], irecv[c], preferred_element_type=jnp.float32
             )
             hid[c, at, :] = (
                 local_out[c, at, :] + entry_rate[at, 0:1] * from_memory
             ).astype(jnp.bfloat16)
-            return carry
-
-        lax.fori_loop(0, rows // TILE, out_tile, 0)
-        for j in range(1, n_head):
-            h = peer(j)
-            put(
-                hid.at[c, pl.ds(pl.multiple_of(h * tok, tok), tok)],
-                ret_ref.at[:, value_cols(head, c)],
-                R + c,
-                (seq, h),
-            )
+            for core in range(2):
+                h = 2 * chip + core
+                pl.when(h != head)(functools.partial(send_hidden, c, h))
         local(hid.at[c, my_rows], ret_ref.at[:, value_cols(head, c)], R + c)
 
     for c in range(CHUNKS):

time: 45.4 us -> 43.3 us (0.954)
  Pallas kernels: 44.2 us -> 42.1 us
    pallas_call x1, Pallas kernels: 44.2 us -> 42.1 us  [per_device(): pl.pallas_call(functools.partial(kernel, (n_seq, n_head)), out_shape=pltp...]
where the time goes in v3:
time: 43.3 us; the launch traced here: 43.2 us
  Pallas kernels  42.1 us (97%)
  other arithmetic  1.07 us (2%)
    pallas_call x1, Pallas kernels, per_device(): pl.pallas_call(functools.partial(kernel, (n_seq, n_head)), out_shape=pltp...  42.1 us
    convert_element_type x1, other arithmetic, per_device(): return gated.astype(bf16)  1.07 us

profile of v3, /device:TPU:129, one launch (start us, length us, event | category | flops | bytes accessed | tf_op | source)
XLA Modules:
  0.0 43.2 jit_solution(12813845366712559412)
XLA Ops:
  0.0 0.0 copy-start
  0.0 42.1 %shard_map.64 = bf16[64,4096]{1,0:T(8,128)(2,1)S(1)} custom-call(bf16[64,2048]{1,0:T(8,128)(2,1)} %q_ref.1, bf16[64,2048]{1,0:T(8,128)(2,1)} %k_ref.1, bf16[64,4096]{1,0:T(8,128)(2,1)} %v_ref.1, f32[1,512]{1,0:T(1,128)} %ig_ref.1, f32[1,512]{1,0:T(1,128)} %fg_ref.1), custom_call_target="tpu_custom_call" | custom-call | tf_op jit(solution)/shard_map/pallas_call | solution.py:453
  42.1 0.0 copy-done
  42.1 1.1 %multiply_convert_fusion = bf16[64,4096]{1,0:T(8,128)(2,1)} fusion(bf16[64,4096]{1,0:T(8,128)(2,1)S(1)} %shard_map.64, bf16[64,4096]{1,0:T(8,128)(2,1)S(1)} %copy-done), kind=kLoop, calls=%fused_computation | loop fusion | flops 1835008 | bytes 1572864 | tf_op jit(solution)/shard_map/convert_element_type | solution.py:464
Async XLA Ops:
  0.0 42.1 %copy-start = (bf16[64,4096]{1,0:T(8,128)(2,1)S(1)}, bf16[64,4096]{1,0:T(8,128)(2,1)}, u32[]{:S(2)}) copy-start(bf16[64,4096]{1,0:T(8,128)(2,1)} %param.11) | copy-start | bytes 1572868

commit v4 on v3

--- a/solution.py
+++ b/solution.py
@@ -12,6 +12,7 @@
 MEMBERS = 16
 CHUNKS = 4
 TILE = 128
+LAG = 1
 PEERS = ((2, 0), (1, 0), (3, 0), (2, 1), (1, 1), (3, 1), (0, 1))
 
 
@@ -37,6 +38,8 @@
     local_out,
     hdr,
     hdr_all,
+    nrm,
+    nrm_all,
     hdr_total,
     hdr_total_all,
     coef_local,
@@ -46,6 +49,7 @@
     mown,
     mrecv,
     usend,
+    umerged,
     urecv,
     isend,
     irecv,
@@ -69,21 +73,34 @@
     head_row = pl.multiple_of(head * tok, tok)
 
     later = n_group - 1
-    K, Q, HDR, GATE = 0, 1, 2, 3
-    V, A, C, R = (4 + CHUNKS * i for i in range(4))
-    HDRT = 4 + 4 * CHUNKS
+    K, Q, HDR, NRM, GATE = range(5)
+    V, A, C, R = (5 + CHUNKS * i for i in range(4))
+    HDRT = 5 + 4 * CHUNKS
     B = HDRT + later
+
+    turned = jnp.where(group == later, MEMBERS // 2, 0)
+    mine = lax.rem(me + turned, MEMBERS)
 
     def member(j):
         return base + lax.rem(me + j, MEMBERS)
 
+    def owner_later(j):
+        turn = jnp.where(group + j == later, MEMBERS // 2, 0)
+        return (group + j) * MEMBERS + lax.rem(me + turn, MEMBERS)
+
     def each_later(act):
         for j in (2, 3, 1):
-            pl.when(group + j < n_group)(functools.partial(act, j, seq + MEMBERS * j))
+            pl.when(group + j < n_group)(functools.partial(act, j, owner_later(j)))
 
     def each_earlier(act):
         for j in range(later):
-            pl.when(j < group)(functools.partial(act, j, j * MEMBERS + me))
+            pl.when(j < group)(functools.partial(act, j, j * MEMBERS + mine))
+
+    def takes(j):
+        return ((group == 1) | (group == 3), group >= 2, group == 3)[j]
+
+    def total_arrived(c, j):
+        arrived(urecv.at[c, j], B + later * c + j)
 
     def peer(j):
         chip, flip = PEERS[j - 1]
@@ -114,15 +131,15 @@
     local(fg_ref, gates.at[1], GATE)
 
     barrier = pltpu.get_barrier_semaphore()
+
+    def greet(j, there):
+        pl.semaphore_signal(barrier, inc=1, device_id=(there, head), device_id_type=MESH)
+
+    each_later(greet)
+    for j in range(1, MEMBERS):
+        pl.semaphore_signal(barrier, inc=1, device_id=(member(j), head), device_id_type=MESH)
     for j in range(1, n_head):
         pl.semaphore_signal(barrier, inc=1, device_id=(seq, peer(j)), device_id_type=MESH)
-    for j in range(1, MEMBERS):
-        pl.semaphore_signal(barrier, inc=1, device_id=(member(j), head), device_id_type=MESH)
-
-    def greet(j, there):
-        pl.semaphore_signal(barrier, inc=1, device_id=(there, head), device_id_type=MESH)
-
-    each_later(greet)
 
     def key_cols(h):
         return pl.ds(pl.multiple_of(h * key_dim, key_dim), key_dim)
@@ -141,6 +158,9 @@
         @pl.when(j >= group)
         def _():
             hdr_total_all[j] = jnp.zeros(hdr_total.shape, jnp.float32)
+
+        @pl.when(jnp.logical_not(takes(j)))
+        def _():
             for c in range(CHUNKS):
                 urecv[c, j] = jnp.zeros(urecv.shape[2:], urecv.dtype)
 
@@ -197,6 +217,11 @@
     hdr[0:1, :] = jnp.broadcast_to(decay, (1, 128))
     hdr[1:2, :] = jnp.broadcast_to(peak_own, (1, 128))
     hdr_total[...] = jnp.zeros_like(hdr_total)
+    nrm[...] = jnp.zeros_like(nrm)
+    hdr_all[me] = hdr[...]
+    for j in range(1, MEMBERS):
+        put(hdr, hdr_all.at[me], HDR, (member(j), head))
+
     arrived(kbuf, K)
 
     def key_tile(i, normal):
@@ -210,10 +235,25 @@
         0, rows // TILE, key_tile, jnp.zeros((1, key_dim), jnp.float32)
     )
     for i in range(key_dim // 128):
-        hdr[2 + i : 3 + i, :] = normal_own[:, i * 128 : (i + 1) * 128]
-    hdr_all[me] = hdr[...]
+        nrm[2 + i : 3 + i, :] = normal_own[:, i * 128 : (i + 1) * 128]
+    nrm_all[me] = nrm[...]
     for j in range(1, MEMBERS):
-        put(hdr, hdr_all.at[me], HDR, (member(j), head))
+        put(nrm, nrm_all.at[me], NRM, (member(j), head))
+
+    norm_rows = slice(2, 2 + key_dim // 128)
+    no_peak = jnp.full((1, 128), NEG_FILL, jnp.float32)
+    no_norm = jnp.zeros((key_dim // 128, 128), jnp.float32)
+
+    arrived(hdr_all.at[pl.ds(0, MEMBERS - 1)], HDR)
+    peak, total = no_peak, jnp.zeros((1, 128), jnp.float32)
+    for g in range(MEMBERS):
+        d, p = hdr_all[g, 0:1, :], hdr_all[g, 1:2, :]
+        new = jnp.maximum(d + peak, p)
+        coef_local[g, 0:1, :] = jnp.exp(d + peak - new)
+        coef_local[g, 1:2, :] = jnp.exp(p - new)
+        peak, total = new, total + d
+    hdr_total[0:1, :] = total
+    hdr_total[1:2, :] = peak
 
     for c in range(CHUNKS):
         arrived(vbuf.at[c], V + c)
@@ -221,26 +261,16 @@
         mown[c] = own.astype(jnp.bfloat16).reshape(MEMBERS, part, width)
         for j in range(1, MEMBERS):
             g = lax.rem(me + j, MEMBERS)
-            put(mown.at[c, g], mrecv.at[c, me], A + c, (base + g, head))
-        mrecv[c, me] = mown[c, me]
-
-    norm_rows = slice(2, 2 + key_dim // 128)
-    no_peak = jnp.full((1, 128), NEG_FILL, jnp.float32)
-    no_norm = jnp.zeros((key_dim // 128, 128), jnp.float32)
-
-    arrived(hdr_all.at[pl.ds(0, MEMBERS - 1)], HDR)
-    peak, norm, total = no_peak, no_norm, jnp.zeros((1, 128), jnp.float32)
+            owned = lax.rem(g + turned, MEMBERS)
+            put(mown.at[c, owned], mrecv.at[c, me], A + c, (base + g, head))
+        mrecv[c, me] = mown[c, mine]
+
+    arrived(nrm_all.at[pl.ds(0, MEMBERS - 1)], NRM)
+    norm = no_norm
     for g in range(MEMBERS):
-        d, p = hdr_all[g, 0:1, :], hdr_all[g, 1:2, :]
-        new = jnp.maximum(d + peak, p)
-        older, newer = jnp.exp(d + peak - new), jnp.exp(p - new)
-        coef_local[g, 0:1, :] = older
-        coef_local[g, 1:2, :] = newer
-        norm = older * norm + newer * hdr_all[g, norm_rows, :]
-        peak, total = new, total + d
-    hdr_total[0:1, :] = total
-    hdr_total[1:2, :] = peak
+        norm = coef_local[g, 0:1, :] * norm + coef_local[g, 1:2, :] * nrm_all[g, norm_rows, :]
     hdr_total[norm_rows, :] = norm
+    hdr_total_all[group] = hdr_total[...]
 
     @pl.when(group < later)
     def _():
@@ -251,7 +281,6 @@
 
     each_later(send_header)
 
-    arrived(qbuf, Q)
     scale = key_dim ** (-0.5)
 
     def score_tile(i, carry):
@@ -261,71 +290,96 @@
         )
         return carry
 
-    lax.fori_loop(0, rows // TILE, score_tile, 0)
-
     def wide(row):
         return jnp.concatenate([row] * (width // 128), axis=1)
 
-    for c in range(CHUNKS):
+    def full_headers():
+        each_earlier(lambda j, there: arrived(hdr_total_all.at[j], HDRT + j))
+        peak, norm = no_peak, no_norm
+        for j in range(n_group - 1):
+            d, p = hdr_total_all[j, 0:1, :], hdr_total_all[j, 1:2, :]
+            new = jnp.maximum(d + peak, p)
+            used = j < group
+            older, newer = jnp.exp(d + peak - new), jnp.exp(p - new)
+            coef_total[j, 0:1, :] = older
+            coef_total[j, 1:2, :] = newer
+            norm = jnp.where(used, older * norm + newer * hdr_total_all[j, norm_rows, :], norm)
+            peak = jnp.where(used, new, peak)
+        for g in range(MEMBERS):
+            entry[g, 1:2, :] = peak
+            entry[g, norm_rows, :] = norm
+            d, p = hdr_all[g, 0:1, :], hdr_all[g, 1:2, :]
+            new = jnp.maximum(d + peak, p)
+            older, newer = jnp.exp(d + peak - new), jnp.exp(p - new)
+            coef_full[g, 0:1, :] = older
+            coef_full[g, 1:2, :] = newer
+            norm = older * norm + newer * nrm_all[g, norm_rows, :]
+            peak = new
+
+    def send_totals(c):
         arrived(mrecv.at[c, pl.ds(0, MEMBERS - 1)], A + c)
-        state = jnp.zeros((part, width), jnp.float32)
-        for g in range(MEMBERS):
-            state = (
-                wide(coef_local[g, 0:1, :]) * state
-                + wide(coef_local[g, 1:2, :]) * mrecv[c, g].astype(jnp.float32)
-            )
-        usend[c] = state.astype(jnp.bfloat16)
-
-        def send_total(j, there):
-            at = B + later * c
-            put(usend.at[c], urecv.at[c, group], at + j - 1, (there, head), at + group)
-
-        each_later(send_total)
-
-    each_earlier(lambda j, there: arrived(hdr_total_all.at[j], HDRT + j))
-    peak, norm = no_peak, no_norm
-    for j in range(n_group - 1):
-        d, p = hdr_total_all[j, 0:1, :], hdr_total_all[j, 1:2, :]
-        new = jnp.maximum(d + peak, p)
-        used = j < group
-        older = jnp.where(used, jnp.exp(d + peak - new), 1.0)
-        newer = jnp.where(used, jnp.exp(p - new), 0.0)
-        coef_total[j, 0:1, :] = older
-        coef_total[j, 1:2, :] = newer
-        norm = jnp.where(used, older * norm + newer * hdr_total_all[j, norm_rows, :], norm)
-        peak = jnp.where(used, new, peak)
-    for g in range(MEMBERS):
-        entry[g, 1:2, :] = peak
-        entry[g, norm_rows, :] = norm
-        d, p = hdr_all[g, 0:1, :], hdr_all[g, 1:2, :]
-        new = jnp.maximum(d + peak, p)
-        older, newer = jnp.exp(d + peak - new), jnp.exp(p - new)
-        coef_full[g, 0:1, :] = older
-        coef_full[g, 1:2, :] = newer
-        norm = older * norm + newer * hdr_all[g, norm_rows, :]
-        peak = new
-
-    for c in range(CHUNKS):
-        each_earlier(lambda j, there: arrived(urecv.at[c, j], B + later * c + j))
-        state = jnp.zeros((part, width), jnp.float32)
-        for j in range(n_group - 1):
-            state = jnp.where(
-                j < group,
-                wide(coef_total[j, 0:1, :]) * state
-                + wide(coef_total[j, 1:2, :]) * urecv[c, j].astype(jnp.float32),
-                state,
-            )
+
+        @pl.when(group < later)
+        def _():
+            state = jnp.zeros((part, width), jnp.float32)
+            for g in range(MEMBERS):
+                state = (
+                    wide(coef_local[g, 0:1, :]) * state
+                    + wide(coef_local[g, 1:2, :]) * mrecv[c, g].astype(jnp.float32)
+                )
+            usend[c] = state.astype(jnp.bfloat16)
+
+            def send_total(src, j):
+                at = B + later * c
+                put(src, urecv.at[c, group], at + j - 1, (owner_later(j), head), at + group)
+
+            pl.when(group == 0)(functools.partial(send_total, usend.at[c], 3))
+            pl.when(group == 1)(functools.partial(send_total, usend.at[c], 2))
+            pl.when(group != 1)(functools.partial(send_total, usend.at[c], 1))
+
+            @pl.when(group == 1)
+            def _():
+                total_arrived(c, 0)
+                umerged[c] = (
+                    wide(coef_total[1, 0:1, :]) * urecv[c, 0].astype(jnp.float32)
+                    + wide(coef_total[1, 1:2, :]) * state
+                ).astype(jnp.bfloat16)
+                send_total(umerged.at[c], 1)
+
+    def send_entering(c):
+        pl.when(group == 3)(functools.partial(total_arrived, c, 0))
+        for j in range(1, later):
+            pl.when(takes(j))(functools.partial(total_arrived, c, j))
+        came = [urecv[c, j].astype(jnp.float32) for j in range(later)]
+        every = came[0]
+        for j in range(1, later):
+            every = wide(coef_total[j, 0:1, :]) * every + wide(coef_total[j, 1:2, :]) * came[j]
+        state = jnp.where(group == 3, every, jnp.where(group == 2, came[1], came[0]))
         for g in range(MEMBERS):
             isend[c, g] = state.astype(jnp.bfloat16)
             state = (
                 wide(coef_full[g, 0:1, :]) * state
                 + wide(coef_full[g, 1:2, :]) * mrecv[c, g].astype(jnp.float32)
             )
-        my_part = pl.ds(pl.multiple_of(me * part, part), part)
+        my_part = pl.ds(pl.multiple_of(mine * part, part), part)
         for j in range(1, MEMBERS):
             g = lax.rem(me + j, MEMBERS)
             put(isend.at[c, g], irecv.at[c, my_part], C + c, (base + g, head))
         irecv[c, my_part] = isend[c, me]
+
+    pl.when(group < 2)(full_headers)
+    for c in range(CHUNKS):
+        send_totals(c)
+        if c >= LAG:
+            pl.when(group < 2)(functools.partial(send_entering, c - LAG))
+    pl.when(group >= 2)(full_headers)
+    for c in range(CHUNKS):
+        if c >= CHUNKS - LAG:
+            send_entering(c)
+        else:
+            pl.when(group >= 2)(functools.partial(send_entering, c))
+    arrived(qbuf, Q)
+    lax.fori_loop(0, rows // TILE, score_tile, 0)
 
     my_entry = entry[me]
     peak_in = my_entry[1:2, 0:1]
@@ -397,11 +451,14 @@
     sent(kbuf.at[peers_rows], K)
     sent(qbuf.at[peers_rows], Q)
     sent(hdr_all.at[pl.ds(0, MEMBERS - 1)], HDR)
+    sent(nrm_all.at[pl.ds(0, MEMBERS - 1)], NRM)
     each_later(lambda j, there: sent(hdr_total, HDRT + j - 1))
     for c in range(CHUNKS):
         sent(vbuf.at[c, peers_rows], V + c)
         sent(mrecv.at[c, pl.ds(0, MEMBERS - 1)], A + c)
-        each_later(lambda j, there: sent(usend.at[c], B + later * c + j - 1))
+        pl.when(group < later)(lambda: sent(usend.at[c], B + later * c))
+        pl.when(group == 1)(lambda: sent(usend.at[c], B + later * c + 1))
+        pl.when(group == 0)(lambda: sent(usend.at[c], B + later * c + 2))
         sent(irecv.at[c, pl.ds(0, key_dim - part)], C + c)
         sent(hid.at[c, peers_rows], R + c)
 
@@ -415,7 +472,7 @@
     part = key_dim // MEMBERS
     n_group = n_seq // MEMBERS
     bf16, f32 = jnp.bfloat16, jnp.float32
-    n_sem = 4 + 4 * CHUNKS + (n_group - 1) * (1 + CHUNKS)
+    n_sem = 5 + 4 * CHUNKS + (n_group - 1) * (1 + CHUNKS)
     scratch = [
         pltpu.VMEM((2, 1, rows), f32),
         pltpu.VMEM((rows, key_dim), bf16),
@@ -432,6 +489,8 @@
         pltpu.VMEM((8, 128), f32),
         pltpu.VMEM((MEMBERS, 8, 128), f32),
         pltpu.VMEM((8, 128), f32),
+        pltpu.VMEM((MEMBERS, 8, 128), f32),
+        pltpu.VMEM((8, 128), f32),
         pltpu.VMEM((n_group, 8, 128), f32),
         pltpu.VMEM((MEMBERS, 8, 128), f32),
         pltpu.VMEM((MEMBERS, 8, 128), f32),
@@ -439,6 +498,7 @@
         pltpu.VMEM((n_group, 8, 128), f32),
         pltpu.VMEM((CHUNKS, MEMBERS, part, width), bf16),
         pltpu.VMEM((CHUNKS, MEMBERS, part, width), bf16),
+        pltpu.VMEM((CHUNKS, part, width), bf16),
         pltpu.VMEM((CHUNKS, part, width), bf16),
         pltpu.VMEM((CHUNKS, n_group, part, width), bf16),
         pltpu.VMEM((CHUNKS, MEMBERS, part, width), bf16),

time: 43.3 us -> 42.2 us (0.975)
  the two profiles are of different devices: /device:TPU:129 before, /device:TPU:289 now
where the time goes in v4:
time: 42.2 us; the launch traced here: 42.1 us
  Pallas kernels  41 us (97%)
  other arithmetic  1.07 us (3%)
    pallas_call x1, Pallas kernels, per_device(): pl.pallas_call(functools.partial(kernel, (n_seq, n_head)), out_shape=pltp...  41 us
    convert_element_type x1, other arithmetic, per_device(): return gated.astype(bf16)  1.07 us

profile of v4, /device:TPU:289, one launch (start us, length us, event | category | flops | bytes accessed | tf_op | source)
XLA Modules:
  0.0 42.1 jit_solution(9009077544846746528)
XLA Ops:
  0.0 0.0 copy-start
  0.0 41.0 %shard_map.64 = bf16[64,4096]{1,0:T(8,128)(2,1)S(1)} custom-call(bf16[64,2048]{1,0:T(8,128)(2,1)} %q_ref.1, bf16[64,2048]{1,0:T(8,128)(2,1)} %k_ref.1, bf16[64,4096]{1,0:T(8,128)(2,1)} %v_ref.1, f32[1,512]{1,0:T(1,128)} %ig_ref.1, f32[1,512]{1,0:T(1,128)} %fg_ref.1), custom_call_target="tpu_custom_call" | custom-call | tf_op jit(solution)/shard_map/pallas_call | solution.py:513
  41.0 0.0 copy-done
  41.0 1.1 %multiply_convert_fusion = bf16[64,4096]{1,0:T(8,128)(2,1)} fusion(bf16[64,4096]{1,0:T(8,128)(2,1)S(1)} %shard_map.64, bf16[64,4096]{1,0:T(8,128)(2,1)S(1)} %copy-done), kind=kLoop, calls=%fused_computation | loop fusion | flops 1835008 | bytes 1572864 | tf_op jit(solution)/shard_map/convert_element_type | solution.py:524
Async XLA Ops:
  0.0 41.0 %copy-start = (bf16[64,4096]{1,0:T(8,128)(2,1)S(1)}, bf16[64,4096]{1,0:T(8,128)(2,1)}, u32[]{:S(2)}) copy-start(bf16[64,4096]{1,0:T(8,128)(2,1)} %param.11) | copy-start | bytes 1572868

commit v5 on v4

--- a/solution.py
+++ b/solution.py
@@ -12,7 +12,7 @@
 MEMBERS = 16
 CHUNKS = 4
 TILE = 128
-LAG = 1
+LAG = 2
 PEERS = ((2, 0), (1, 0), (3, 0), (2, 1), (1, 1), (3, 1), (0, 1))
 
 
@@ -178,10 +178,6 @@
         for j in range(1, n_head):
             h = peer(j)
             put(v_ref.at[:, value_cols(h, c)], vbuf.at[c, my_rows], V + c, (seq, h))
-    for j in range(1, n_head):
-        h = peer(j)
-        put(q_ref.at[:, key_cols(h)], qbuf.at[my_rows], Q, (seq, h))
-
     arrived(gates, GATE)
     gate = gates[0]
     forget = gates[1]
@@ -264,6 +260,10 @@
             owned = lax.rem(g + turned, MEMBERS)
             put(mown.at[c, owned], mrecv.at[c, me], A + c, (base + g, head))
         mrecv[c, me] = mown[c, mine]
+        if c == CHUNKS - 2:
+            for j in range(1, n_head):
+                h = peer(j)
+                put(q_ref.at[:, key_cols(h)], qbuf.at[my_rows], Q, (seq, h))
 
     arrived(nrm_all.at[pl.ds(0, MEMBERS - 1)], NRM)
     norm = no_norm
@@ -373,13 +373,14 @@
         if c >= LAG:
             pl.when(group < 2)(functools.partial(send_entering, c - LAG))
     pl.when(group >= 2)(full_headers)
+    arrived(qbuf, Q)
+    pl.when(group == 3)(lambda: lax.fori_loop(0, rows // TILE, score_tile, None))
     for c in range(CHUNKS):
         if c >= CHUNKS - LAG:
             send_entering(c)
         else:
             pl.when(group >= 2)(functools.partial(send_entering, c))
-    arrived(qbuf, Q)
-    lax.fori_loop(0, rows // TILE, score_tile, 0)
+    pl.when(group < 3)(lambda: lax.fori_loop(0, rows // TILE, score_tile, None))
 
     my_entry = entry[me]
     peak_in = my_entry[1:2, 0:1]

time: 42.2 us -> 41.9 us (level)
  the two profiles are of different devices: /device:TPU:289 before, /device:TPU:385 now
where the time goes in v5:
time: 41.9 us; the launch traced here: 41.8 us
  Pallas kernels  40.7 us (97%)
  other arithmetic  1.07 us (3%)
    pallas_call x1, Pallas kernels, per_device(): pl.pallas_call(functools.partial(kernel, (n_seq, n_head)), out_shape=pltp...  40.7 us
    convert_element_type x1, other arithmetic, per_device(): return gated.astype(bf16)  1.07 us

profile of v5, /device:TPU:385, one launch (start us, length us, event | category | flops | bytes accessed | tf_op | source)
XLA Modules:
  0.0 41.8 jit_solution(14336281489077166126)
XLA Ops:
  0.0 0.0 copy-start
  0.0 40.7 %shard_map.64 = bf16[64,4096]{1,0:T(8,128)(2,1)S(1)} custom-call(bf16[64,2048]{1,0:T(8,128)(2,1)} %q_ref.1, bf16[64,2048]{1,0:T(8,128)(2,1)} %k_ref.1, bf16[64,4096]{1,0:T(8,128)(2,1)} %v_ref.1, f32[1,512]{1,0:T(1,128)} %ig_ref.1, f32[1,512]{1,0:T(1,128)} %fg_ref.1), custom_call_target="tpu_custom_call" | custom-call | tf_op jit(solution)/shard_map/pallas_call | solution.py:514
  40.7 0.0 copy-done
  40.7 1.1 %multiply_convert_fusion = bf16[64,4096]{1,0:T(8,128)(2,1)} fusion(bf16[64,4096]{1,0:T(8,128)(2,1)S(1)} %shard_map.64, bf16[64,4096]{1,0:T(8,128)(2,1)S(1)} %copy-done), kind=kLoop, calls=%fused_computation | loop fusion | flops 1835008 | bytes 1572864 | tf_op jit(solution)/shard_map/convert_element_type | solution.py:525
Async XLA Ops:
  0.0 40.7 %copy-start = (bf16[64,4096]{1,0:T(8,128)(2,1)S(1)}, bf16[64,4096]{1,0:T(8,128)(2,1)}, u32[]{:S(2)}) copy-start(bf16[64,4096]{1,0:T(8,128)(2,1)} %param.11) | copy-start | bytes 1572868

commit v6 on v5

--- a/solution.py
+++ b/solution.py
@@ -11,6 +11,7 @@
 NEG_FILL = -1e30
 MEMBERS = 16
 CHUNKS = 4
+ROW = 4
 TILE = 128
 LAG = 2
 PEERS = ((2, 0), (1, 0), (3, 0), (2, 1), (1, 1), (3, 1), (0, 1))
@@ -57,6 +58,7 @@
     send_sem,
     recv_sem,
     relay_sem,
+    row_sem,
 ):
     n_seq, n_head = sizes
     n_group = n_seq // MEMBERS
@@ -136,8 +138,11 @@
         pl.semaphore_signal(barrier, inc=1, device_id=(there, head), device_id_type=MESH)
 
     each_later(greet)
-    for j in range(1, MEMBERS):
+    for j in range(ROW, MEMBERS, ROW):
         pl.semaphore_signal(barrier, inc=1, device_id=(member(j), head), device_id_type=MESH)
+    for j in range(1, ROW):
+        beside = base + me - lax.rem(me, ROW) + lax.rem(me + j, ROW)
+        pl.semaphore_signal(barrier, inc=1, device_id=(beside, head), device_id_type=MESH)
     for j in range(1, n_head):
         pl.semaphore_signal(barrier, inc=1, device_id=(seq, peer(j)), device_id_type=MESH)
 
@@ -164,7 +169,11 @@
             for c in range(CHUNKS):
                 urecv[c, j] = jnp.zeros(urecv.shape[2:], urecv.dtype)
 
-    pl.semaphore_wait(barrier, n_head - 1 + MEMBERS - 1 + group)
+    rows_apart = MEMBERS // ROW - 1
+    pl.semaphore_wait(barrier, n_head - 1 + rows_apart + ROW - 1 + group)
+
+    for j in range(ROW, MEMBERS, ROW):
+        pl.semaphore_signal(row_sem, inc=1, device_id=(member(j), head), device_id_type=MESH)
 
     def answer(j, there):
         pl.semaphore_signal(relay_sem, inc=1, device_id=(there, head), device_id_type=MESH)
@@ -215,6 +224,7 @@
     hdr_total[...] = jnp.zeros_like(hdr_total)
     nrm[...] = jnp.zeros_like(nrm)
     hdr_all[me] = hdr[...]
+    pl.semaphore_wait(row_sem, rows_apart)
     for j in range(1, MEMBERS):
         put(hdr, hdr_all.at[me], HDR, (member(j), head))
 
@@ -508,6 +518,7 @@
         pltpu.SemaphoreType.DMA((n_sem,)),
         pltpu.SemaphoreType.DMA((n_sem,)),
         pltpu.SemaphoreType.REGULAR,
+        pltpu.SemaphoreType.REGULAR,
     ]
     anywhere = pl.BlockSpec(memory_space=pl.ANY)
     hbm = pl.BlockSpec(memory_space=pltpu.HBM)

time: 41.9 us -> 41.7 us (level)
  no operation moved by 1% of the time
where the time goes in v6:
time: 41.7 us; the launch traced here: 41.6 us
  Pallas kernels  40.5 us (97%)
  other arithmetic  1.07 us (3%)
    pallas_call x1, Pallas kernels, per_device(): pl.pallas_call(functools.partial(kernel, (n_seq, n_head)), out_shape=pltp...  40.5 us
    convert_element_type x1, other arithmetic, per_device(): return gated.astype(bf16)  1.07 us

profile of v6, /device:TPU:385, one launch (start us, length us, event | category | flops | bytes accessed | tf_op | source)
XLA Modules:
  0.0 41.6 jit_solution(14378169325674896830)
XLA Ops:
  0.0 0.0 copy-start
  0.0 40.5 %shard_map.64 = bf16[64,4096]{1,0:T(8,128)(2,1)S(1)} custom-call(bf16[64,2048]{1,0:T(8,128)(2,1)} %q_ref.1, bf16[64,2048]{1,0:T(8,128)(2,1)} %k_ref.1, bf16[64,4096]{1,0:T(8,128)(2,1)} %v_ref.1, f32[1,512]{1,0:T(1,128)} %ig_ref.1, f32[1,512]{1,0:T(1,128)} %fg_ref.1), custom_call_target="tpu_custom_call" | custom-call | tf_op jit(solution)/shard_map/pallas_call | solution.py:525
  40.5 0.0 copy-done
  40.5 1.1 %multiply_convert_fusion = bf16[64,4096]{1,0:T(8,128)(2,1)} fusion(bf16[64,4096]{1,0:T(8,128)(2,1)S(1)} %shard_map.64, bf16[64,4096]{1,0:T(8,128)(2,1)S(1)} %copy-done), kind=kLoop, calls=%fused_computation | loop fusion | flops 1835008 | bytes 1572864 | tf_op jit(solution)/shard_map/convert_element_type | solution.py:536
Async XLA Ops:
  0.0 40.5 %copy-start = (bf16[64,4096]{1,0:T(8,128)(2,1)S(1)}, bf16[64,4096]{1,0:T(8,128)(2,1)}, u32[]{:S(2)}) copy-start(bf16[64,4096]{1,0:T(8,128)(2,1)} %param.11) | copy-start | bytes 1572868
